TPU v7x, 256 devices: a whole 4x4x8 slice. The times are simulated.
256 devices in a mesh: row: 32 (over y, x, core), col: 8 (over z).
Axes of the slice: x: 4, y: 4, z: 8, core: 2. Of those that a mesh axis runs over, the one named last changes fastest.
Arguments:
- queries: bfloat16 [16384, 3072], P('row', 'col'), may hold values from -6 to 6
- keys_in: bfloat16 [16384, 3072], P('row', 'col'), may hold values from -6 to 6
- values_in: bfloat16 [16384, 3072], P('row', 'col'), may hold values from -6 to 6
- query_gain: float32 [3072], P('col'), may hold values from 0.1 to 1.9
- key_gain: float32 [3072], P('col'), may hold values from 0.1 to 1.9
- out_weight: bfloat16 [3072, 6144], P('row', 'col'), may hold values from -0.109375 to 0.109375
- cotangent: bfloat16 [16384, 6144], P('row', 'col'), may hold values from -6 to 6
Outputs:
- output: bfloat16 [16384, 6144], P('row', 'col')
- grad_queries: bfloat16 [16384, 3072], P('row', 'col')
- grad_keys: bfloat16 [16384, 3072], P('row', 'col')
- grad_values: bfloat16 [16384, 3072], P('row', 'col')
- grad_weight: bfloat16 [3072, 6144], P('row', 'col')
All inputs are finite; a program needn't handle non-finite values.
Results may differ from a plain program's by a relative error of at most 0.0087.
Values may be sent and summed in bfloat16 or wider, within the bound.
A program may use at most 128 MiB of HBM per device.

v0:
```python
import jax
import jax.numpy as jnp
from jax import lax
from jax.sharding import PartitionSpec as P

HEAD_DIM = 128
PATCHES = 256


epsilon = 1e-06


def head_norm(inside, scaling):
    average = jnp.mean(inside, axis=-1, keepdims=True)
    centred = inside - average
    spread = jnp.mean(centred * centred, axis=-1, keepdims=True)
    return centred * lax.rsqrt(spread + epsilon) * scaling


def product(pattern, first_op, second_op):
    return jnp.einsum(pattern, first_op, second_op, preferred_element_type=jnp.float32)


def attend(queries, keys_in, values_in, query_gains, key_gains):
    score_scale = queries.shape[-1] ** (-0.5)
    query_norm = head_norm(queries.astype(jnp.float32), query_gains).astype(jnp.bfloat16)
    key_norm = head_norm(keys_in.astype(jnp.float32), key_gains).astype(jnp.bfloat16)
    scores = product("nqhd,nkhd->nhqk", query_norm, key_norm) * score_scale
    weights = jnp.exp(scores)
    probabilities = weights / jnp.sum(weights, axis=-1, keepdims=True)
    prob_low = probabilities.astype(jnp.bfloat16)
    attended = product("nhqk,nkhd->nqhd", prob_low, values_in).astype(jnp.bfloat16)
    return (query_norm, key_norm, probabilities, prob_low, attended)


def attend_back(
    queries,
    keys_in,
    values_in,
    query_gains,
    key_gains,
    query_norm,
    key_norm,
    probabilities,
    prob_low,
    grad_attended,
):
    score_scale = queries.shape[-1] ** (-0.5)
    grad_probs = product("nqhd,nkhd->nhqk", grad_attended, values_in)
    inner_sum = jnp.sum(probabilities * grad_probs, axis=-1, keepdims=True)
    grad_scores = (probabilities * (grad_probs - inner_sum) * score_scale).astype(jnp.bfloat16)
    grad_values = product("nhqk,nqhd->nkhd", prob_low, grad_attended).astype(jnp.bfloat16)
    grad_qnorm = product("nhqk,nkhd->nqhd", grad_scores, key_norm)
    grad_knorm = product("nhqk,nqhd->nkhd", grad_scores, query_norm)
    unused, query_pull = jax.vjp(
        lambda inside: head_norm(inside, query_gains), queries.astype(jnp.float32)
    )
    unused, key_pull = jax.vjp(
        lambda inside: head_norm(inside, key_gains), keys_in.astype(jnp.float32)
    )
    grad_queries = query_pull(grad_qnorm)[0].astype(jnp.bfloat16)
    grad_keys = key_pull(grad_knorm)[0].astype(jnp.bfloat16)
    return (grad_queries, grad_keys, grad_values)


def per_device(queries, keys_in, values_in, query_gain, key_gain, out_weight, cotangent):
    tok_rows, head_cols = queries.shape
    heads_here = head_cols // HEAD_DIM
    image_shape = (tok_rows // PATCHES, PATCHES, heads_here, HEAD_DIM)
    query_gains = query_gain.reshape(heads_here, HEAD_DIM)
    key_gains = key_gain.reshape(heads_here, HEAD_DIM)
    query_blocks = queries.reshape(image_shape)
    key_blocks = keys_in.reshape(image_shape)
    value_blocks = values_in.reshape(image_shape)
    stored = attend(query_blocks, key_blocks, value_blocks, query_gains, key_gains)
    attended = stored[4].reshape(tok_rows, head_cols)
    mixed_panel = lax.all_gather(attended, "col", axis=1, tiled=True)
    columns = mixed_panel
    out_sum = jnp.dot(
        columns,
        lax.all_gather(out_weight, "row", axis=0, tiled=True),
        preferred_element_type=jnp.float32,
    )
    grad_terms = lax.dot_general(
        cotangent,
        lax.all_gather(out_weight, "row", axis=0, tiled=True),
        (((1,), (1,)), ((), ())),
        preferred_element_type=jnp.float32,
    )
    output = out_sum.astype(jnp.bfloat16)
    grad_attended = lax.psum_scatter(grad_terms, "col", scatter_dimension=1, tiled=True).astype(
        jnp.bfloat16
    )
    columns = mixed_panel
    grad_weight = lax.psum_scatter(
        lax.dot_general(
            columns, cotangent, (((0,), (0,)), ((), ())), preferred_element_type=jnp.float32
        ),
        "row",
        scatter_dimension=0,
        tiled=True,
    ).astype(jnp.bfloat16)
    gradients = attend_back(
        query_blocks,
        key_blocks,
        value_blocks,
        query_gains,
        key_gains,
        stored[0],
        stored[1],
        stored[2],
        stored[3],
        grad_attended.reshape(image_shape),
    )
    flat_shape = (tok_rows, head_cols)
    return (
        output,
        gradients[0].reshape(flat_shape),
        gradients[1].reshape(flat_shape),
        gradients[2].reshape(flat_shape),
        grad_weight,
    )


def solution(mesh):
    placed = (
        P("row", "col"),
        P("row", "col"),
        P("row", "col"),
        P("col"),
        P("col"),
        P("row", "col"),
        P("row", "col"),
    )
    return jax.shard_map(
        per_device,
        mesh=mesh,
        in_specs=placed,
        out_specs=(
            P("row", "col"),
            P("row", "col"),
            P("row", "col"),
            P("row", "col"),
            P("row", "col"),
        ),
        check_vma=False,
    )
```

profile of v0, /device:TPU:1, one launch (start us, length us, event | category | flops | bytes accessed | tf_op | source)
XLA Modules:
  0.0 336.8 jit_solution(8336577730308215185)
XLA Ops:
  7.2 0.0 all-gather.3.cloned.1.call-start
  7.2 1.5 reshape.97
  8.7 1.2 copy.76
  9.9 0.5 reshape.92
  10.4 0.3 reduce_sum.86
  10.7 0.1 multiply_reduce_fusion.4
  10.8 0.0 copy-done.6
  10.9 1.1 copy.81
  11.9 1.6 reshape.93
  13.6 0.3 reduce_sum.91
  13.9 0.1 multiply_reduce_fusion.3
  14.0 1.0 multiply_convert_fusion.1
  15.0 2.9 fusion.25
  17.9 2.6 fusion.22
  20.4 1.5 copy.91
  21.9 0.8 copy.129
  22.7 0.0 all-gather.3.cloned.1.call-update
  22.8 0.0 all-gather.5.cloned.1.call-start
  22.8 0.7 all-gather.5.cloned.1.call-update
  23.5 0.0 reduce-scatter.5.cloned.1.call-start
  23.6 47.9 %all-gather.3.cloned.1.call-done = bf16[512,3072]{0,1:T(8,128)(2,1)} async-done(((bf16[512,384]{0,1:T(8,128)(2,1)}), bf16[512,3072]{0,1:T(8,128)(2,1)}) %all-gather.3.cloned.1.call-update) | async-done | bytes 3145744 | tf_op jit(solution)/shard_map/all_gather | solution.py:77
  71.5 8.1 %fusion.52 = f32[3072,768]{1,0:T(8,128)} fusion(bf16[512,3072]{0,1:T(8,128)(2,1)} %all-gather.3.cloned.1.call-done, bf16[512,768]{1,0:T(8,128)(2,1)S(1)} %copy-done), kind=kOutput, calls=%fused_computation.63 | convolution fusion | flops 2415919104 | bytes 13369344 | tf_op jit(solution)/shard_map/dot_general | solution.py:96
  79.6 0.0 reduce-scatter.5.cloned.1.call-update
  79.6 0.2 reduce-scatter.3.cloned.1.call-start
  79.8 45.3 %all-gather.5.cloned.1.call-done = bf16[3072,768]{1,0:T(8,128)(2,1)} async-done(((bf16[96,768]{1,0:T(8,128)(2,1)}), bf16[3072,768]{1,0:T(8,128)(2,1)}) %all-gather.5.cloned.1.call-update) | async-done | bytes 4718608 | tf_op jit(solution)/shard_map/all_gather | solution.py:81
  125.2 6.9 %fusion.51 = f32[512,3072]{1,0:T(8,128)} fusion(bf16[512,768]{1,0:T(8,128)(2,1)S(1)} %copy-done, bf16[3072,768]{1,0:T(8,128)(2,1)} %all-gather.5.cloned.1.call-done), kind=kOutput, calls=%fused_computation.62 | convolution fusion | flops 2415919104 | bytes 11796480 | tf_op jit(solution)/shard_map/dot_general | solution.py:84
  132.0 0.0 reduce-scatter.3.cloned.1.call-update
  132.0 6.8 %convolution_convert_fusion = bf16[512,768]{1,0:T(8,128)(2,1)} fusion(bf16[512,3072]{0,1:T(8,128)(2,1)} %all-gather.3.cloned.1.call-done, bf16[3072,768]{1,0:T(8,128)(2,1)} %all-gather.5.cloned.1.call-done), kind=kOutput, calls=%fused_computation.7 | convolution fusion | flops 2416312320 | bytes 8650752 | tf_op jit(solution)/shard_map/dot_general | solution.py:79
  138.9 90.9 %reduce-scatter.5.cloned.1.call-done = f32[96,768]{1,0:T(8,128)} async-done(((f32[3072,768]{1,0:T(8,128)}), f32[96,768]{1,0:T(8,128)}) %reduce-scatter.5.cloned.1.call-update) | async-done | bytes 294928 | tf_op jit(solution)/shard_map/reduce_scatter | solution.py:95
  229.7 1.6 convert_element_type.69
  231.4 77.2 %reduce-scatter.3.cloned.1.call-done = f32[512,384]{1,0:T(8,128)} async-done(((f32[512,3072]{1,0:T(8,128)}), f32[512,384]{1,0:T(8,128)}) %reduce-scatter.3.cloned.1.call-update) | async-done | bytes 786448 | tf_op jit(solution)/shard_map/reduce_scatter | solution.py:91
  308.5 1.2 convert_element_type.63
  309.7 0.9 reshape.98
  310.6 1.2 copy.107
  311.9 2.6 fusion.23
  314.4 1.5 fusion.30
  315.9 4.6 %multiply_reduce_fusion.2 = (f32[2,256,3]{1,2,0:T(4,128)S(1)}, f32[2,256,3,128]{1,3,2,0:T(8,128)}) fusion(f32[2,256,3,128]{1,0,3,2:T(2,128)S(1)} %reshape.92, f32[2,256,3]{1,2,0:T(4,128)S(1)} %copy.77, f32[3,128]{1,0:T(4,128)S(1)} %bitcast.55, bf16[2,256,3,128]{1,3,2,0:T(8,128)(2,1)} %get-tuple-element.24, f32[2,3,256,256]{2,3,1,0:T(8,128)} %fusion.25, ...), kind=kOutput, calls=%fused_computation.23 | convolution fusion | flops 103416064 | bytes 5125632 | tf_op jit(solution)/shard_map/nhqk,nkhd->nqhd/dot_general | solution.py:21
  320.5 4.4 %multiply_reduce_fusion.1 = (f32[2,256,3]{1,2,0:T(4,128)S(1)}, f32[2,256,3,128]{1,3,2,0:T(8,128)}) fusion(f32[2,256,3,128]{1,0,3,2:T(2,128)S(1)} %reshape.93, f32[2,256,3]{1,2,0:T(4,128)S(1)} %copy.82, f32[3,128]{1,0:T(4,128)S(1)} %bitcast.57, bf16[2,256,3,128]{1,3,2,0:T(8,128)(2,1)S(1)} %copy-done.5, f32[2,3,256,256]{2,3,1,0:T(8,128)} %fusion.25, ...), kind=kOutput, calls=%fused_computation.21 | convolution fusion | flops 103416064 | bytes 5125632 | tf_op jit(solution)/shard_map/nhqk,nqhd->nkhd/dot_general | solution.py:21
  324.9 0.3 copy.121
  325.2 0.8 copy.188
  326.1 1.4 fusion.34
  327.5 0.2 add_convert_fusion
  327.7 0.2 fusion.33
  327.9 0.2 add_convert_fusion.1
  328.1 0.3 copy.119
  328.3 0.8 copy.190
  329.2 0.3 copy.120
  329.4 0.8 copy.189
  (31 shorter events, 0.1 us)
Async XLA Ops:
  7.2 64.3 %copy-start = (bf16[512,768]{1,0:T(8,128)(2,1)S(1)}, bf16[512,768]{1,0:T(8,128)(2,1)}, u32[]{:S(2)}) copy-start(bf16[512,768]{1,0:T(8,128)(2,1)} %param.13) | copy-start | bytes 2359300
  7.2 64.3 %all-gather.3.cloned.1.call-start = ((), (), s32[]{:S(2)}) async-start(), calls=%async_computation.2 | async-start | bytes 3538944 | tf_op jit(solution)/shard_map/all_gather | solution.py:77
  9.9 1.0 copy-start.6
  11.9 2.1 copy-start.7
  11.9 2.1 copy-start.8
  15.0 2.9 copy-start.4
  22.8 102.4 %all-gather.5.cloned.1.call-start = ((), (), s32[]{:S(2)}) async-start(), calls=%async_computation.3 | async-start | bytes 4866048 | tf_op jit(solution)/shard_map/all_gather | solution.py:81
  23.5 206.2 %reduce-scatter.5.cloned.1.call-start = ((), (), s32[]{:S(2)}) async-start(), calls=%async_computation.5 | async-start | bytes 9732096 | tf_op jit(solution)/shard_map/reduce_scatter | solution.py:95
  79.6 228.9 %reduce-scatter.3.cloned.1.call-start = ((), (), s32[]{:S(2)}) async-start(), calls=%async_computation.4 | async-start | bytes 7077888 | tf_op jit(solution)/shard_map/reduce_scatter | solution.py:91
  315.9 4.6 %copy-start.5 = (bf16[2,256,3,128]{1,3,2,0:T(8,128)(2,1)S(1)}, bf16[2,256,3,128]{1,3,2,0:T(8,128)(2,1)}, u32[]{:S(2)}) copy-start(bf16[2,256,3,128]{1,3,2,0:T(8,128)(2,1)} %copy-done.4) | copy-start | bytes 1179652
  320.5 4.4 %copy-start.3 = (bf16[2,256,3,128]{1,3,2,0:T(8,128)(2,1)S(1)}, bf16[2,256,3,128]{1,3,2,0:T(8,128)(2,1)}, u32[]{:S(2)}) copy-start(bf16[2,256,3,128]{1,3,2,0:T(8,128)(2,1)} %fusion.23) | copy-start | bytes 1179652
  325.2 2.3 copy-start.2
  326.1 1.6 copy-start.1
Sparse Core Ops, SparseCore 0:
  22.9 48.5 all-gather.2
  74.0 51.1 all-gather.4
  129.2 100.4 reduce-scatter.4
  232.3 76.1 reduce-scatter.2
where the time goes:
time: 337 us
  waiting for transfers between devices  262 us (78%)
  matrix products  40.3 us (12%)
  between operations  14 us (4%)
  local copies, waits for them, and re-layouts  13.6 us (4%)
  other arithmetic  6.51 us (2%)
    reduce_scatter x1, waiting for transfers between devices, per_device(): lax.psum_scatter(lax.dot_general(columns, cotangent, (((0,), (0,)), ((),...  90.9 us
    reduce_scatter x1, waiting for transfers between devices, per_device(): lax.psum_scatter(grad_terms, 'col', scatter_dimension=1, tiled=True)  77.2 us
    all_gather x1, waiting for transfers between devices, per_device(): mixed_panel = lax.all_gather(attended, 'col', axis=1, tiled=True)  47.9 us
    all_gather x1, waiting for transfers between devices, per_device(): lax.all_gather(out_weight, 'row', axis=0, tiled=True)  45.3 us
    dot_general x5, matrix products, product(): jnp.einsum(pattern, first_op, second_op, preferred_element_type=jnp.float32)  15.6 us
    dot_general x1, matrix products, per_device(): lax.dot_general(columns, cotangent, (((0,), (0,)), ((), ())), preferred_e...  8.13 us
    dot_general x1, matrix products, per_device(): lax.dot_general(cotangent, lax.all_gather(out_weight, 'row', axis=0, tile...  6.85 us
    dot_general x1, matrix products, per_device(): jnp.dot(columns, lax.all_gather(out_weight, 'row', axis=0, tiled=True), p...  6.83 us
  transfers between devices with their start and end apart: 4, of which 4 were waited for; matrix products, arithmetic and copies ran while one was open for 7% of the time, Pallas kernels for 0%

commit v1 on v0

v1 whole, which is shorter than its diff:
```python
import jax
import jax.numpy as jnp
from jax import lax
from jax.experimental import pallas as pl
from jax.experimental.pallas import tpu as pltpu
from jax.sharding import PartitionSpec as P

HEAD_DIM = 128
PATCHES = 256
HEADS_HERE = 3
NX, NY, NZ = 4, 4, 8
SHARD_ROWS = 96
HALF_ROWS = 48
HALF_COLS = 384
EPSILON = 1e-06
MESH = pl.DeviceIdType.MESH
BF16 = jnp.bfloat16
F32 = jnp.float32


def dot_nn(a, b):
    return jnp.dot(a, b, preferred_element_type=F32)


def dot_nt(a, b):
    return lax.dot_general(a, b, (((1,), (1,)), ((), ())), preferred_element_type=F32)


def dot_tn(a, b):
    return lax.dot_general(a, b, (((0,), (0,)), ((), ())), preferred_element_type=F32)


def block_kernel(
    q_ref, k_ref, v_ref, qg_ref, kg_ref, w_ref, ct_ref,
    out_ref, gq_ref, gk_ref, gv_ref, gw_ref,
    wall, aall, prob, plow, qhat, khat, qrs, krs, qn, kn,
    gsend, grecv, gwb, sib, s1, r1, s2, r2, c1,
    w1_send, w1_recv, w2_send, w2_recv, ws0_send, ws0_recv, ws1_send, ws1_recv, ws2_send, ws2_recv,
    a_send, a_recv, g_send, g_recv, sib_send, sib_recv, p1_send, p1_recv, p2_send, p2_recv,
):
    row = lax.axis_index("row")
    z = lax.axis_index("col")
    core = lax.rem(row, 2)
    x = lax.rem(lax.div(row, 2), NX)
    y = lax.div(row, 2 * NX)
    scale = HEAD_DIM ** (-0.5)

    def device(yy, xx, cc, zz):
        return ((yy * NX + xx) * 2 + cc, zz)

    def x_turn(j):
        return device(y, lax.rem(x + 1 + 2 * j, NX), core, z)

    def y_turn(j):
        return device(lax.rem(y + 1 + 2 * j, NY), x, core, z)

    def z_turn(image):
        return (row, lax.rem(z + 1 + 6 * image, NZ))

    sibling = device(y, x, 1 - core, z)

    barrier = pltpu.get_barrier_semaphore()
    for peer in (x_turn(0), x_turn(1), y_turn(0), y_turn(1), z_turn(0), z_turn(1), sibling):
        pl.semaphore_signal(barrier, inc=1, device_id=peer, device_id_type=MESH)
    pl.semaphore_wait(barrier, 7)

    def remote(src, dst, send, recv, peer):
        return pltpu.make_async_remote_copy(
            src_ref=src, dst_ref=dst, send_sem=send, recv_sem=recv, device_id=peer, device_id_type=MESH
        )

    def behind(pos, steps, j):
        return lax.rem(pos + (4 - steps if j == 0 else steps), 4)

    def w1_ref(i, j, steps):
        if i == 0:
            return wall.at[j, y, behind(x, steps, j), core, i]
        return wall.at[j, behind(y, steps, j), x, core, i]

    def w2_ref(i, j, steps):
        if i == 0:
            return wall.at[j, behind(y, steps, j), :, core, i]
        return wall.at[j, :, behind(x, steps, j), core, i]

    def w1_copy(i, j, s):
        ref = w1_ref(i, j, s)
        return remote(ref, ref, w1_send.at[i, j, s], w1_recv.at[i, j, s], x_turn(j) if i == 0 else y_turn(j))

    def w2_copy(i, j, s):
        ref = w2_ref(i, j, s)
        return remote(ref, ref, w2_send.at[i, j, s], w2_recv.at[i, j, s], y_turn(j) if i == 0 else x_turn(j))

    def ws0_copy():
        ref = wall.at[:, y, x, core]
        return remote(ref, ref, ws0_send, ws0_recv, sibling)

    def ws1_copy(i, j, s):
        ref = w1_ref(i, j, s + 1)
        return remote(ref, ref, ws1_send.at[i, j, s], ws1_recv.at[i, j, s], sibling)

    def ws2_copy(i, j, s):
        ref = w2_ref(i, j, s + 1)
        return remote(ref, ref, ws2_send.at[i, j, s], ws2_recv.at[i, j, s], sibling)

    quarters = [(i, j) for i in range(2) for j in range(2)]

    def weight_step(t):
        for i, j in quarters:
            if t < 3:
                w1_copy(i, j, t).wait_recv()
                if t < 2:
                    w1_copy(i, j, t + 1).start()
                else:
                    w2_copy(i, j, 0).start()
                ws1_copy(i, j, t).start()
            else:
                w2_copy(i, j, t - 3).wait_recv()
                if t < 5:
                    w2_copy(i, j, t - 2).start()
                ws2_copy(i, j, t - 3).start()

    def weight_wait():
        ws0_copy().wait_recv()
        for i, j in quarters:
            for s in range(3):
                ws1_copy(i, j, s).wait_recv()
                ws2_copy(i, j, s).wait_recv()

    def weight_sent():
        ws0_copy().wait_send()
        for i, j in quarters:
            for s in range(3):
                w1_copy(i, j, s).wait_send()
                w2_copy(i, j, s).wait_send()
                ws1_copy(i, j, s).wait_send()
                ws2_copy(i, j, s).wait_send()

    def a_copy(image, s, h):
        origin = lax.rem(z + (NZ - s if image == 0 else s), NZ)
        ref = aall.at[origin * HEADS_HERE + h, pl.ds(image * PATCHES, PATCHES)]
        return remote(ref, ref, a_send.at[image, s, h], a_recv.at[image, s, h], z_turn(image))

    def a_pass(s, h):
        for image in range(2):
            a_copy(image, s - 1, h).wait_recv()
            a_copy(image, s, h).start()

    def head_slice(image, h):
        return (pl.ds(image * PATCHES, PATCHES), pl.ds(pl.multiple_of(h * HEAD_DIM, HEAD_DIM), HEAD_DIM))

    def norm_forward(image, h, source, gain, hat, spread_ref, normed):
        inside = source[head_slice(image, h)].astype(F32)
        centred = inside - jnp.mean(inside, axis=-1, keepdims=True)
        spread = jnp.mean(centred * centred, axis=-1, keepdims=True)
        factor = lax.rsqrt(spread + EPSILON)
        unit = centred * factor
        hat[image, h] = unit
        spread_ref[image, h] = jnp.broadcast_to(factor, unit.shape)
        value = (unit * gain[h]).astype(BF16)
        normed[image, h] = value
        return value

    def forward(image, h):
        q_norm = norm_forward(image, h, q_ref, qg_ref, qhat, qrs, qn)
        k_norm = norm_forward(image, h, k_ref, kg_ref, khat, krs, kn)
        weights = jnp.exp(dot_nt(q_norm, k_norm) * scale)
        probabilities = weights * (1.0 / jnp.sum(weights, axis=-1, keepdims=True))
        low = probabilities.astype(BF16)
        prob[image, h] = probabilities
        plow[image, h] = low
        attended = dot_nn(low, v_ref[head_slice(image, h)]).astype(BF16)
        aall[z * HEADS_HERE + h, pl.ds(image * PATCHES, PATCHES)] = attended

    def norm_backward(grad, image, h, gain, hat, spread_ref):
        scaled = grad * gain[h]
        unit = hat[image, h]
        first = jnp.mean(scaled, axis=-1, keepdims=True)
        second = jnp.mean(scaled * unit, axis=-1, keepdims=True)
        return (spread_ref[image, h] * (scaled - first - unit * second)).astype(BF16)

    def backward(image, h, grad_attended):
        place = head_slice(image, h)
        probabilities = prob[image, h]
        gv_ref[place] = dot_tn(plow[image, h], grad_attended).astype(BF16)
        grad_probs = dot_nt(grad_attended, v_ref[place])
        inner = jnp.sum(probabilities * grad_probs, axis=-1, keepdims=True)
        grad_scores = (probabilities * (grad_probs - inner) * scale).astype(BF16)
        grad_q = dot_nn(grad_scores, kn[image, h])
        grad_k = dot_tn(grad_scores, qn[image, h])
        gq_ref[place] = norm_backward(grad_q, image, h, qg_ref, qhat, qrs)
        gk_ref[place] = norm_backward(grad_k, image, h, kg_ref, khat, krs)

    def weight_rows(j, o):
        piece = wall[j, lax.div(o, 2), pl.ds(2 * lax.rem(o, 2), 2)]
        return piece.reshape(HEADS_HERE * HEAD_DIM, HALF_COLS)

    def g_copy(image, s, h):
        return remote(
            gsend.at[image, s, h], grecv.at[image, s, h], g_send.at[image, s, h], g_recv.at[image, s, h], z_turn(image)
        )

    def g_term(image, s):
        owner = lax.rem(z + (2 * NZ - 1 - s if image == 0 else 1 + s), NZ)
        rows = pl.ds(image * PATCHES, PATCHES)
        return dot_nt(ct_ref[rows, :HALF_COLS], weight_rows(0, owner)) + dot_nt(
            ct_ref[rows, HALF_COLS:], weight_rows(1, owner)
        )

    def head_columns(value, h):
        return value[:, h * HEAD_DIM : (h + 1) * HEAD_DIM]

    def g_first():
        for image in range(2):
            term = g_term(image, 0)
            for h in range(HEADS_HERE):
                gsend[image, 0, h] = head_columns(term, h).astype(BF16)
                g_copy(image, 0, h).start()

    def g_step(s):
        terms = [g_term(image, s) for image in range(2)]
        for h in range(HEADS_HERE):
            for image in range(2):
                g_copy(image, s - 1, h).wait_recv()
                total = head_columns(terms[image], h) + grecv[image, s - 1, h].astype(F32)
                gsend[image, s, h] = total.astype(BF16)
                g_copy(image, s, h).start()

    def gw_copy(index, o):
        place = pl.ds(2 * lax.rem(o, 2), 2)
        return remote(
            gwb.at[1 - core, lax.div(o, 2), place],
            sib.at[lax.div(o, 2), place],
            sib_send.at[index],
            sib_recv.at[index],
            sibling,
        )

    def gw_block(index, o):
        panel = jnp.concatenate([aall[o * HEADS_HERE + h] for h in range(HEADS_HERE)], axis=1)
        for j in range(2):
            value = dot_tn(panel, ct_ref[:, j * HALF_COLS : (j + 1) * HALF_COLS]).astype(BF16)
            for xx in range(2):
                for cc in range(2):
                    for i in range(2):
                        at = (xx * 4 + cc * 2 + i) * HALF_ROWS
                        gwb[cc, lax.div(o, 2), 2 * lax.rem(o, 2) + xx, i, j] = value[at : at + HALF_ROWS]
        gw_copy(index, o).start()

    def gw_owner(index):
        return lax.rem(z + index, NZ)

    def chip_sum(i, j, d):
        if i == 0:
            return gwb[core, :, d, i, j].astype(F32) + sib[:, d, i, j].astype(F32)
        return gwb[core, d, :, i, j].astype(F32) + sib[d, :, i, j].astype(F32)

    def p1_copy(i, j, s):
        peer = x_turn(j) if i == 0 else y_turn(j)
        return remote(s1.at[i, j, s], r1.at[i, j, s], p1_send.at[i, j, s], p1_recv.at[i, j, s], peer)

    def p2_copy(i, j, s):
        peer = y_turn(j) if i == 0 else x_turn(j)
        return remote(s2.at[i, j, s], r2.at[i, j, s], p2_send.at[i, j, s], p2_recv.at[i, j, s], peer)

    def scatter_step(t):
        for i, j in quarters:
            first, second = (x, y) if i == 0 else (y, x)
            if t <= 3:
                total = chip_sum(i, j, behind(first, (1 + t) % 4, j))
                if t > 0:
                    p1_copy(i, j, t - 1).wait_recv()
                    total = total + r1[i, j, t - 1].astype(F32)
                if t < 3:
                    s1[i, j, t] = total.astype(BF16)
                    p1_copy(i, j, t).start()
                else:
                    c1[i, j] = total
                    s2[i, j, 0] = c1[i, j, behind(second, 1, j)].astype(BF16)
                    p2_copy(i, j, 0).start()
            else:
                s = t - 4
                p2_copy(i, j, s).wait_recv()
                total = c1[i, j, behind(second, (2 + s) % 4, j)] + r2[i, j, s].astype(F32)
                if s < 2:
                    s2[i, j, s + 1] = total.astype(BF16)
                    p2_copy(i, j, s + 1).start()
                else:
                    gw_ref[
                        i * HALF_ROWS : (i + 1) * HALF_ROWS, j * HALF_COLS : (j + 1) * HALF_COLS
                    ] = total.astype(BF16)

    def output_part(image, j):
        rows = pl.ds(pl.multiple_of(image * PATCHES, PATCHES), PATCHES)
        total = None
        for o in range(NZ):
            panel = jnp.concatenate([aall[o * HEADS_HERE + h, rows] for h in range(HEADS_HERE)], axis=1)
            term = dot_nn(panel, weight_rows(j, o))
            total = term if total is None else total + term
        out_ref[rows, j * HALF_COLS : (j + 1) * HALF_COLS] = total.astype(BF16)

    for i, j in quarters:
        wall[j, y, x, core, i] = w_ref[
            i * HALF_ROWS : (i + 1) * HALF_ROWS, j * HALF_COLS : (j + 1) * HALF_COLS
        ]
    for i, j in quarters:
        w1_copy(i, j, 0).start()
    ws0_copy().start()

    def forward_loop(h, carry):
        for image in range(2):
            forward(image, h)
            a_copy(image, 0, h).start()
        for t in range(3):
            @pl.when(h == t)
            def _():
                weight_step(t)

        @pl.when(h >= 1)
        def _():
            a_pass(1, h - 1)

        return carry

    lax.fori_loop(0, HEADS_HERE, forward_loop, 0)
    a_pass(1, HEADS_HERE - 1)

    gw_block(0, gw_owner(0))

    def gather_loop(s, carry):
        for h in range(HEADS_HERE):
            a_pass(s, h)
        for t in range(3, 6):
            @pl.when(s == t - 1)
            def _():
                weight_step(t)

        @pl.when(s == 4)
        def _():
            gw_block(4, gw_owner(4))

        @pl.when(s >= 5)
        def _():
            def both(side, inner):
                index = jnp.where(side == 0, 8 - s, s)
                gw_block(index, gw_owner(index))
                return inner

            lax.fori_loop(0, 2, both, 0)

        return carry

    lax.fori_loop(2, 7, gather_loop, 0)
    weight_wait()
    g_first()
    for h in range(HEADS_HERE):
        for image in range(2):
            a_copy(image, 6, h).wait_recv()

    def last_two(side, carry):
        index = 1 + 6 * side
        gw_block(index, gw_owner(index))
        return carry

    lax.fori_loop(0, 2, last_two, 0)

    def reduce_loop(s, carry):
        g_step(s)

        @pl.when(s == 1)
        def _():
            for index in range(NZ):
                gw_copy(index, gw_owner(index)).wait_recv()

        for t in range(6):
            @pl.when(s == t + 1)
            def _():
                scatter_step(t)

        @pl.when(jnp.logical_and(s >= 2, s < 4))
        def _():
            for j in range(2):
                output_part(s - 2, j)

        return carry

    lax.fori_loop(1, 7, reduce_loop, 0)

    terms = [g_term(image, 7) for image in range(2)]
    for h in range(HEADS_HERE):
        for image in range(2):
            gsend[image, 7, h] = head_columns(terms[image], h).astype(BF16)

    def backward_loop(h, carry):
        for image in range(2):
            g_copy(image, 6, h).wait_recv()
            grad_attended = (gsend[image, 7, h].astype(F32) + grecv[image, 6, h].astype(F32)).astype(BF16)
            backward(image, h, grad_attended)

        @pl.when(h == 0)
        def _():
            scatter_step(6)

        return carry

    lax.fori_loop(0, HEADS_HERE, backward_loop, 0)

    weight_sent()
    for i, j in quarters:
        for s in range(3):
            p1_copy(i, j, s).wait_send()
            p2_copy(i, j, s).wait_send()
    for index in range(NZ):
        gw_copy(index, gw_owner(index)).wait_send()

    def sent_loop(s, carry):
        for h in range(HEADS_HERE):
            for image in range(2):
                a_copy(image, s, h).wait_send()
                g_copy(image, s, h).wait_send()
        return carry

    lax.fori_loop(0, 7, sent_loop, 0)


def per_device(queries, keys_in, values_in, query_gain, key_gain, out_weight, cotangent):
    dma = pltpu.SemaphoreType.DMA
    unit = (2, HEADS_HERE, PATCHES, HEAD_DIM)
    square = (2, HEADS_HERE, PATCHES, PATCHES)
    quarter = (HALF_ROWS, HALF_COLS)
    scratch = [
        pltpu.VMEM((2, NY, NX, 2, 2) + quarter, BF16),
        pltpu.VMEM((NZ * HEADS_HERE, 2 * PATCHES, HEAD_DIM), BF16),
        pltpu.VMEM(square, F32),
        pltpu.VMEM(square, BF16),
        pltpu.VMEM(unit, F32),
        pltpu.VMEM(unit, F32),
        pltpu.VMEM(unit, F32),
        pltpu.VMEM(unit, F32),
        pltpu.VMEM(unit, BF16),
        pltpu.VMEM(unit, BF16),
        pltpu.VMEM((2, 8, HEADS_HERE, PATCHES, HEAD_DIM), BF16),
        pltpu.VMEM((2, 7, HEADS_HERE, PATCHES, HEAD_DIM), BF16),
        pltpu.VMEM((2, NY, NX, 2, 2) + quarter, BF16),
        pltpu.VMEM((NY, NX, 2, 2) + quarter, BF16),
        pltpu.VMEM((2, 2, 3, 4) + quarter, BF16),
        pltpu.VMEM((2, 2, 3, 4) + quarter, BF16),
        pltpu.VMEM((2, 2, 3) + quarter, BF16),
        pltpu.VMEM((2, 2, 3) + quarter, BF16),
        pltpu.VMEM((2, 2, 4) + quarter, F32),
    ]
    ring4, ring8 = (2, 2, 3), (2, 7, HEADS_HERE)
    scratch += [dma(ring4), dma(ring4), dma(ring4), dma(ring4), dma, dma]
    scratch += [dma(ring4), dma(ring4), dma(ring4), dma(ring4)]
    scratch += [dma(ring8), dma(ring8), dma(ring8), dma(ring8), dma((NZ,)), dma((NZ,))]
    scratch += [dma(ring4), dma(ring4), dma(ring4), dma(ring4)]
    vmem = pl.BlockSpec(memory_space=pltpu.VMEM)
    gain_shape = (HEADS_HERE, 1, HEAD_DIM)
    tokens, features = queries.shape
    results = [
        jax.ShapeDtypeStruct(cotangent.shape, BF16),
        jax.ShapeDtypeStruct((tokens, features), BF16),
        jax.ShapeDtypeStruct((tokens, features), BF16),
        jax.ShapeDtypeStruct((tokens, features), BF16),
        jax.ShapeDtypeStruct(out_weight.shape, BF16),
    ]
    return pl.pallas_call(
        block_kernel,
        out_shape=results,
        in_specs=[vmem] * 7,
        out_specs=[vmem] * 5,
        scratch_shapes=scratch,
        compiler_params=pltpu.CompilerParams(
            collective_id=0, has_side_effects=True, vmem_limit_bytes=60 * 1024 * 1024
        ),
        cost_estimate=pl.CostEstimate(flops=8_000_000_000, bytes_accessed=4_200_000, transcendentals=400_000),
    )(
        queries,
        keys_in,
        values_in,
        query_gain.reshape(gain_shape),
        key_gain.reshape(gain_shape),
        out_weight,
        cotangent,
    )


def solution(mesh):
    placed = (
        P("row", "col"),
        P("row", "col"),
        P("row", "col"),
        P("col"),
        P("col"),
        P("row", "col"),
        P("row", "col"),
    )
    return jax.shard_map(
        per_device,
        mesh=mesh,
        in_specs=placed,
        out_specs=(P("row", "col"),) * 5,
        check_vma=False,
    )
```

time: 337 us -> 96.7 us (0.29)
  waiting for transfers between devices: 262 us -> 0 us
  Pallas kernels: 0 us -> 86.3 us
  matrix products: 40.3 us -> 0 us
  between operations: 14 us -> 0.66 us
  other arithmetic: 6.51 us -> 0 us
  local copies, waits for them, and re-layouts: 13.6 us -> 7.92 us
    reduce_scatter x2 -> x0, waiting for transfers between devices: 168 us -> none  [the longest x1 90.9 us: per_device(): lax.psum_scatter(lax.dot_general(columns, cotangent, (((0,), (0,)), ((),...]
    all_gather x2 -> x0, waiting for transfers between devices: 93.2 us -> none  [the longest x1 47.9 us: per_device(): mixed_panel = lax.all_gather(attended, 'col', axis=1, tiled=True)]
    pallas_call x0 -> x1, Pallas kernels: none -> 86.3 us  [per_device(): pl.pallas_call(block_kernel, out_shape=results, in_specs=[vmem] * 7, out_...]
    dot_general x8 -> x0, matrix products: 37.4 us -> none  [the longest x5 15.6 us: product(): jnp.einsum(pattern, first_op, second_op, preferred_element_type=jnp.float32)]
    convert_element_type x5 -> x0, local copies, waits for them, and re-layouts: 5.86 us -> none  [the longest x2 2.72 us: attend(): keys_in.astype(jnp.float32)]
    convert_element_type x5 -> x0, other arithmetic: 4.13 us -> none  [the longest x1 1.64 us: per_device(): grad_weight = lax.psum_scatter(lax.dot_general(columns, cotangent, (((0,)...]
  transfers between devices with their start and end apart: 4 -> 0, of which waited for: 4 -> 0; matrix products, arithmetic and copies ran while one was open for 7% -> 0% of each run, Pallas kernels for 0% -> 0%
where the time goes in v1:
time: 96.7 us; the launch traced here: 94.9 us
  Pallas kernels  86.3 us (89%)
  local copies, waits for them, and re-layouts  7.92 us (8%)
    pallas_call x1, Pallas kernels, per_device(): pl.pallas_call(block_kernel, out_shape=results, in_specs=[vmem] * 7, out_...  86.3 us
    unnamed x15, local copies, waits for them, and re-layouts  6.08 us

profile of v1, /device:TPU:1, one launch (start us, length us, event | category | flops | bytes accessed | tf_op | source)
XLA Modules:
  0.0 94.9 jit_solution(3808935077303911157)
XLA Ops:
  0.6 0.0 copy-start.4
  0.6 1.3 %reshape.16.qg_ref = f32[3,1,128]{2,1,0:T(1,128)} reshape(f32[384]{0:T(512)} %param.10) | data formatting | bytes 3072 | tf_op jit(solution)/shard_map/reshape | solution.py:480
  1.9 0.0 copy-done.4
  1.9 0.6 reshape.17.kg_ref
  2.5 86.3 %shard_map.110 = (bf16[512,768]{1,0:T(8,128)(2,1)}, bf16[512,384]{1,0:T(8,128)(2,1)}, bf16[512,384]{1,0:T(8,128)(2,1)}, bf16[512,384]{1,0:T(8,128)(2,1)}, bf16[96,768]{1,0:T(8,128)(2,1)}) custom-call(bf16[512,384]{1,0:T(8,128)(2,1)} %q_ref.1, bf16[512,384]{1,0:T(8,128)(2,1)} %k_ref.1, bf16[512,384]{1,0:T(8,128)(2,1)} %v_ref.1, f32[3,1,128]{2,1,0:T(1,128)} %reshape.16.qg_ref, ...), custom_call_target="tpu_custom_call" | custom-call | flops 8000000000 | bytes 4200000 | tf_op jit(solution)/shard_map/pallas_call | solution.py:466
  88.8 0.0 copy-start.2
  88.8 2.1 %copy.17 = bf16[512,768]{1,0:T(8,128)(2,1)} copy(bf16[512,768]{1,0:T(8,128)(2,1)} %get-tuple-element.10) | data formatting | bytes 1572864
  90.9 0.0 copy-done.2
  90.9 0.0 copy-start.1
  90.9 0.7 copy.18
  91.7 0.4 copy-done.1
  92.1 0.0 copy-start
  92.1 0.7 copy.19
  92.8 0.4 copy-done
  93.2 0.0 copy-start.3
  93.2 0.7 copy.20
  94.0 0.3 copy-done.3
  94.2 0.7 copy.21
Async XLA Ops:
  0.6 1.3 %copy-start.4 = (f32[384]{0:T(512)S(1)}, f32[384]{0:T(512)}, u32[]{:S(2)}) copy-start(f32[384]{0:T(512)} %param.11) | copy-start | bytes 4612
  88.8 2.1 %copy-start.2 = (bf16[512,384]{1,0:T(8,128)(2,1)S(1)}, bf16[512,384]{1,0:T(8,128)(2,1)}, u32[]{:S(2)}) copy-start(bf16[512,384]{1,0:T(8,128)(2,1)} %get-tuple-element.11) | copy-start | bytes 1179652
  90.9 1.1 %copy-start.1 = (bf16[512,384]{1,0:T(8,128)(2,1)S(1)}, bf16[512,384]{1,0:T(8,128)(2,1)}, u32[]{:S(2)}) copy-start(bf16[512,384]{1,0:T(8,128)(2,1)} %get-tuple-element.12) | copy-start | bytes 1179652
  92.1 1.1 %copy-start = (bf16[512,384]{1,0:T(8,128)(2,1)S(1)}, bf16[512,384]{1,0:T(8,128)(2,1)}, u32[]{:S(2)}) copy-start(bf16[512,384]{1,0:T(8,128)(2,1)} %get-tuple-element.13) | copy-start | bytes 1179652
  93.2 1.0 %copy-start.3 = (bf16[96,768]{1,0:T(8,128)(2,1)S(1)}, bf16[96,768]{1,0:T(8,128)(2,1)}, u32[]{:S(2)}) copy-start(bf16[96,768]{1,0:T(8,128)(2,1)} %get-tuple-element.14) | copy-start | bytes 442372

commit v2 on v1

--- a/solution.py
+++ b/solution.py
@@ -12,6 +12,10 @@
 SHARD_ROWS = 96
 HALF_ROWS = 48
 HALF_COLS = 384
+TILE_ROWS = 128
+PART_SLOTS = (((2, 5), (6, 7)), ((7, 8), (9, 12)))
+PART_SHIFT = (3, 8)
+STORE_PARTS = 2
 EPSILON = 1e-06
 MESH = pl.DeviceIdType.MESH
 BF16 = jnp.bfloat16
@@ -31,10 +35,13 @@
 
 
 def block_kernel(
-    q_ref, k_ref, v_ref, qg_ref, kg_ref, w_ref, ct_ref,
+    q_in, k_in, v_in, qg_in, kg_in, w_in, ct_in,
+    out_hbm, gq_hbm, gk_hbm, gv_hbm, gw_hbm,
+    q_ref, k_ref, v_ref, w_ref, ct_ref, qg_ref, kg_ref,
     out_ref, gq_ref, gk_ref, gv_ref, gw_ref,
     wall, aall, prob, plow, qhat, khat, qrs, krs, qn, kn,
-    gsend, grecv, gwb, sib, s1, r1, s2, r2, c1,
+    gsend, grecv, gterm, gwb, sib, s1, r1, s2, r2, c1,
+    load_sem, out_sem, grad_sem, gw_sem,
     w1_send, w1_recv, w2_send, w2_recv, ws0_send, ws0_recv, ws1_send, ws1_recv, ws2_send, ws2_recv,
     a_send, a_recv, g_send, g_recv, sib_send, sib_recv, p1_send, p1_recv, p2_send, p2_recv,
 ):
@@ -62,7 +69,18 @@
     barrier = pltpu.get_barrier_semaphore()
     for peer in (x_turn(0), x_turn(1), y_turn(0), y_turn(1), z_turn(0), z_turn(1), sibling):
         pl.semaphore_signal(barrier, inc=1, device_id=peer, device_id_type=MESH)
-    pl.semaphore_wait(barrier, 7)
+
+    loads = [
+        pltpu.make_async_copy(source, target, load_sem.at[n])
+        for n, (source, target) in enumerate(
+            ((q_in, q_ref), (k_in, k_ref), (v_in, v_ref), (w_in, w_ref), (ct_in, ct_ref))
+        )
+    ]
+    for load in loads:
+        load.start()
+    for h in range(HEADS_HERE):
+        qg_ref[h, 0] = qg_in[h * HEAD_DIM : (h + 1) * HEAD_DIM]
+        kg_ref[h, 0] = kg_in[h * HEAD_DIM : (h + 1) * HEAD_DIM]
 
     def remote(src, dst, send, recv, peer):
         return pltpu.make_async_remote_copy(
@@ -215,15 +233,6 @@
             for h in range(HEADS_HERE):
                 gsend[image, 0, h] = head_columns(term, h).astype(BF16)
                 g_copy(image, 0, h).start()
-
-    def g_step(s):
-        terms = [g_term(image, s) for image in range(2)]
-        for h in range(HEADS_HERE):
-            for image in range(2):
-                g_copy(image, s - 1, h).wait_recv()
-                total = head_columns(terms[image], h) + grecv[image, s - 1, h].astype(F32)
-                gsend[image, s, h] = total.astype(BF16)
-                g_copy(image, s, h).start()
 
     def gw_copy(index, o):
         place = pl.ds(2 * lax.rem(o, 2), 2)
@@ -289,31 +298,51 @@
                         i * HALF_ROWS : (i + 1) * HALF_ROWS, j * HALF_COLS : (j + 1) * HALF_COLS
                     ] = total.astype(BF16)
 
-    def output_part(image, j):
-        rows = pl.ds(pl.multiple_of(image * PATCHES, PATCHES), PATCHES)
+    def output_copy(tile):
+        rows = pl.ds(pl.multiple_of(tile * TILE_ROWS, TILE_ROWS), TILE_ROWS)
+        return pltpu.make_async_copy(out_ref.at[rows], out_hbm.at[rows], out_sem.at[tile])
+
+    def output_part(tile, j):
+        rows = pl.ds(pl.multiple_of(tile * TILE_ROWS, TILE_ROWS), TILE_ROWS)
         total = None
         for o in range(NZ):
             panel = jnp.concatenate([aall[o * HEADS_HERE + h, rows] for h in range(HEADS_HERE)], axis=1)
             term = dot_nn(panel, weight_rows(j, o))
             total = term if total is None else total + term
         out_ref[rows, j * HALF_COLS : (j + 1) * HALF_COLS] = total.astype(BF16)
-
+        if j == 1:
+            output_copy(tile).start()
+
+    def grad_copies(h):
+        columns = pl.ds(pl.multiple_of(h * HEAD_DIM, HEAD_DIM), HEAD_DIM)
+        return [
+            pltpu.make_async_copy(source.at[:, columns], target.at[:, columns], grad_sem.at[n, h])
+            for n, (source, target) in enumerate(((gq_ref, gq_hbm), (gk_ref, gk_hbm), (gv_ref, gv_hbm)))
+        ]
+
+    loads[3].wait()
     for i, j in quarters:
         wall[j, y, x, core, i] = w_ref[
             i * HALF_ROWS : (i + 1) * HALF_ROWS, j * HALF_COLS : (j + 1) * HALF_COLS
         ]
+    for load in loads[:3]:
+        load.wait()
+    pl.semaphore_wait(barrier, 7)
     for i, j in quarters:
         w1_copy(i, j, 0).start()
     ws0_copy().start()
+
+    def at_slot(slot, moments, action):
+        for t, moment in moments:
+            @pl.when(slot == moment)
+            def _():
+                action(t)
 
     def forward_loop(h, carry):
         for image in range(2):
             forward(image, h)
             a_copy(image, 0, h).start()
-        for t in range(3):
-            @pl.when(h == t)
-            def _():
-                weight_step(t)
+        at_slot(h, ((0, 1), (1, 2)), weight_step)
 
         @pl.when(h >= 1)
         def _():
@@ -322,87 +351,95 @@
         return carry
 
     lax.fori_loop(0, HEADS_HERE, forward_loop, 0)
+    loads[4].wait()
     a_pass(1, HEADS_HERE - 1)
-
     gw_block(0, gw_owner(0))
 
-    def gather_loop(s, carry):
-        for h in range(HEADS_HERE):
-            a_pass(s, h)
-        for t in range(3, 6):
-            @pl.when(s == t - 1)
-            def _():
-                weight_step(t)
-
-        @pl.when(s == 4)
+    def gather_loop(slot, carry):
+        a_pass(2 + lax.div(slot, HEADS_HERE), lax.rem(slot, HEADS_HERE))
+        at_slot(slot, ((2, 0), (3, 4), (4, 8), (5, 12)), weight_step)
+
+        @pl.when(jnp.logical_or(slot == 9, jnp.logical_or(slot == 11, jnp.logical_or(slot == 13, slot == 14))))
         def _():
-            gw_block(4, gw_owner(4))
-
-        @pl.when(s >= 5)
-        def _():
-            def both(side, inner):
-                index = jnp.where(side == 0, 8 - s, s)
-                gw_block(index, gw_owner(index))
-                return inner
-
-            lax.fori_loop(0, 2, both, 0)
+            index = jnp.where(slot == 9, 4, jnp.where(slot == 11, 3, jnp.where(slot == 13, 5, 2)))
+            gw_block(index, gw_owner(index))
 
         return carry
 
-    lax.fori_loop(2, 7, gather_loop, 0)
+    lax.fori_loop(0, 5 * HEADS_HERE, gather_loop, 0)
     weight_wait()
     g_first()
     for h in range(HEADS_HERE):
         for image in range(2):
             a_copy(image, 6, h).wait_recv()
 
-    def last_two(side, carry):
-        index = 1 + 6 * side
+    def last_three(n, carry):
+        index = jnp.where(n == 0, 6, jnp.where(n == 1, 1, 7))
         gw_block(index, gw_owner(index))
         return carry
 
-    lax.fori_loop(0, 2, last_two, 0)
-
-    def reduce_loop(s, carry):
-        g_step(s)
-
-        @pl.when(s == 1)
+    lax.fori_loop(0, 3, last_three, 0)
+
+    def reduce_loop(slot, carry):
+        s, h = 1 + lax.div(slot, HEADS_HERE), lax.rem(slot, HEADS_HERE)
+
+        @pl.when(h == 0)
+        def _():
+            for image in range(2):
+                term = g_term(image, s)
+                for head in range(HEADS_HERE):
+                    gterm[image, head] = head_columns(term, head)
+
+        for image in range(2):
+            g_copy(image, s - 1, h).wait_recv()
+            total = gterm[image, h] + grecv[image, s - 1, h].astype(F32)
+            gsend[image, s, h] = total.astype(BF16)
+            g_copy(image, s, h).start()
+
+        @pl.when(slot == 1)
         def _():
             for index in range(NZ):
                 gw_copy(index, gw_owner(index)).wait_recv()
 
-        for t in range(6):
-            @pl.when(s == t + 1)
+        at_slot(slot, ((0, 1), (1, 5), (2, 8), (3, 12), (4, 14), (5, 16)), scatter_step)
+        for j in range(2):
+
+            @pl.when(jnp.logical_or(*[jnp.logical_and(slot >= a, slot < b) for a, b in PART_SLOTS[j]]))
             def _():
-                scatter_step(t)
-
-        @pl.when(jnp.logical_and(s >= 2, s < 4))
-        def _():
-            for j in range(2):
-                output_part(s - 2, j)
+                output_part(slot - jnp.where(slot >= PART_SLOTS[j][1][0], PART_SHIFT[j], PART_SLOTS[j][0][0]), j)
 
         return carry
 
-    lax.fori_loop(1, 7, reduce_loop, 0)
-
-    terms = [g_term(image, 7) for image in range(2)]
-    for h in range(HEADS_HERE):
-        for image in range(2):
-            gsend[image, 7, h] = head_columns(terms[image], h).astype(BF16)
+    lax.fori_loop(0, 6 * HEADS_HERE, reduce_loop, 0)
+
+    for image in range(2):
+        term = g_term(image, 7)
+        for head in range(HEADS_HERE):
+            gterm[image, head] = head_columns(term, head)
 
     def backward_loop(h, carry):
         for image in range(2):
             g_copy(image, 6, h).wait_recv()
-            grad_attended = (gsend[image, 7, h].astype(F32) + grecv[image, 6, h].astype(F32)).astype(BF16)
+            grad_attended = (gterm[image, h] + grecv[image, 6, h].astype(F32)).astype(BF16)
             backward(image, h, grad_attended)
+        for copy in grad_copies(h):
+            copy.start()
 
         @pl.when(h == 0)
         def _():
             scatter_step(6)
+            gw_result = pltpu.make_async_copy(gw_ref, gw_hbm, gw_sem)
+            gw_result.start()
 
         return carry
 
     lax.fori_loop(0, HEADS_HERE, backward_loop, 0)
+    for h in range(HEADS_HERE):
+        for copy in grad_copies(h):
+            copy.wait()
+    pltpu.make_async_copy(gw_ref, gw_hbm, gw_sem).wait()
+    for tile in range(4):
+        output_copy(tile).wait()
 
     weight_sent()
     for i, j in quarters:
@@ -422,12 +459,39 @@
     lax.fori_loop(0, 7, sent_loop, 0)
 
 
+def store_kernel(*refs):
+    made, results, held, load_sem, store_sem = refs[:5], refs[5:10], refs[10:15], refs[15], refs[16]
+    parts = [(n, part) for n in range(5) for part in range(STORE_PARTS)]
+
+    def piece(ref, part):
+        rows = ref.shape[0] // STORE_PARTS
+        return ref.at[pl.ds(part * rows, rows)]
+
+    loads = [
+        pltpu.make_async_copy(piece(made[n], part), piece(held[n], part), load_sem.at[n, part]) for n, part in parts
+    ]
+    stores = [
+        pltpu.make_async_copy(piece(held[n], part), piece(results[n], part), store_sem.at[n, part])
+        for n, part in parts
+    ]
+    for load in loads:
+        load.start()
+    for load, store in zip(loads, stores):
+        load.wait()
+        store.start()
+    for store in stores:
+        store.wait()
+
+
 def per_device(queries, keys_in, values_in, query_gain, key_gain, out_weight, cotangent):
     dma = pltpu.SemaphoreType.DMA
     unit = (2, HEADS_HERE, PATCHES, HEAD_DIM)
     square = (2, HEADS_HERE, PATCHES, PATCHES)
     quarter = (HALF_ROWS, HALF_COLS)
-    scratch = [
+    scratch = [pltpu.VMEM(a.shape, BF16) for a in (queries, keys_in, values_in, out_weight, cotangent)]
+    scratch += [pltpu.VMEM((HEADS_HERE, 1, HEAD_DIM), F32)] * 2
+    scratch += [pltpu.VMEM(a.shape, BF16) for a in (cotangent, queries, queries, queries, out_weight)]
+    scratch += [
         pltpu.VMEM((2, NY, NX, 2, 2) + quarter, BF16),
         pltpu.VMEM((NZ * HEADS_HERE, 2 * PATCHES, HEAD_DIM), BF16),
         pltpu.VMEM(square, F32),
@@ -438,8 +502,9 @@
         pltpu.VMEM(unit, F32),
         pltpu.VMEM(unit, BF16),
         pltpu.VMEM(unit, BF16),
-        pltpu.VMEM((2, 8, HEADS_HERE, PATCHES, HEAD_DIM), BF16),
         pltpu.VMEM((2, 7, HEADS_HERE, PATCHES, HEAD_DIM), BF16),
+        pltpu.VMEM((2, 7, HEADS_HERE, PATCHES, HEAD_DIM), BF16),
+        pltpu.VMEM(unit, F32),
         pltpu.VMEM((2, NY, NX, 2, 2) + quarter, BF16),
         pltpu.VMEM((NY, NX, 2, 2) + quarter, BF16),
         pltpu.VMEM((2, 2, 3, 4) + quarter, BF16),
@@ -449,12 +514,13 @@
         pltpu.VMEM((2, 2, 4) + quarter, F32),
     ]
     ring4, ring8 = (2, 2, 3), (2, 7, HEADS_HERE)
+    scratch += [dma((5,)), dma((4,)), dma((3, HEADS_HERE)), dma]
     scratch += [dma(ring4), dma(ring4), dma(ring4), dma(ring4), dma, dma]
     scratch += [dma(ring4), dma(ring4), dma(ring4), dma(ring4)]
     scratch += [dma(ring8), dma(ring8), dma(ring8), dma(ring8), dma((NZ,)), dma((NZ,))]
     scratch += [dma(ring4), dma(ring4), dma(ring4), dma(ring4)]
     vmem = pl.BlockSpec(memory_space=pltpu.VMEM)
-    gain_shape = (HEADS_HERE, 1, HEAD_DIM)
+    anywhere = pl.BlockSpec(memory_space=pl.ANY)
     tokens, features = queries.shape
     results = [
         jax.ShapeDtypeStruct(cotangent.shape, BF16),
@@ -463,25 +529,27 @@
         jax.ShapeDtypeStruct((tokens, features), BF16),
         jax.ShapeDtypeStruct(out_weight.shape, BF16),
     ]
-    return pl.pallas_call(
+    made = pl.pallas_call(
         block_kernel,
         out_shape=results,
-        in_specs=[vmem] * 7,
-        out_specs=[vmem] * 5,
+        in_specs=[anywhere] * 3 + [vmem] * 2 + [anywhere] * 2,
+        out_specs=[anywhere] * 5,
         scratch_shapes=scratch,
         compiler_params=pltpu.CompilerParams(
             collective_id=0, has_side_effects=True, vmem_limit_bytes=60 * 1024 * 1024
         ),
         cost_estimate=pl.CostEstimate(flops=8_000_000_000, bytes_accessed=4_200_000, transcendentals=400_000),
     )(
-        queries,
-        keys_in,
-        values_in,
-        query_gain.reshape(gain_shape),
-        key_gain.reshape(gain_shape),
-        out_weight,
-        cotangent,
+        queries, keys_in, values_in, query_gain, key_gain, out_weight, cotangent
     )
+    return pl.pallas_call(
+        store_kernel,
+        out_shape=results,
+        in_specs=[anywhere] * 5,
+        out_specs=[anywhere] * 5,
+        scratch_shapes=[pltpu.VMEM(a.shape, a.dtype) for a in results] + [dma((5, STORE_PARTS))] * 2,
+        compiler_params=pltpu.CompilerParams(vmem_limit_bytes=60 * 1024 * 1024),
+    )(*made)
 
 
 def solution(mesh):

time: 96.7 us -> 84.6 us (0.87)
  local copies, waits for them, and re-layouts: 7.92 us -> 0 us
  Pallas kernels: 86.3 us -> 82.4 us
    unnamed x15 -> x0, local copies, waits for them, and re-layouts: 6.08 us -> none
    pallas_call x1 -> x2, Pallas kernels: 86.3 us -> 82.4 us  [the longest x1 80 us: per_device(): pl.pallas_call(block_kernel, out_shape=results, in_specs=[anywhere] * 3 +...]
    reshape x2 -> x0, local copies, waits for them, and re-layouts: 1.84 us -> none  [the longest x1 1.26 us: per_device(): query_gain.reshape(gain_shape)]
where the time goes in v2:
time: 84.6 us; the launch traced here: 83.1 us
  Pallas kernels  82.4 us (97%)
    pallas_call x1, Pallas kernels, per_device(): pl.pallas_call(block_kernel, out_shape=results, in_specs=[anywhere] * 3 +...  80 us
    pallas_call x1, Pallas kernels, per_device(): pl.pallas_call(store_kernel, out_shape=results, in_specs=[anywhere] * 5,...  2.48 us

profile of v2, /device:TPU:1, one launch (start us, length us, event | category | flops | bytes accessed | tf_op | source)
XLA Modules:
  0.0 83.1 jit_solution(11545513438175898597)
XLA Ops:
  0.6 80.0 %shard_map.110 = (bf16[512,768]{1,0:T(8,128)(2,1)}, bf16[512,384]{1,0:T(8,128)(2,1)}, bf16[512,384]{1,0:T(8,128)(2,1)}, bf16[512,384]{1,0:T(8,128)(2,1)}, bf16[96,768]{1,0:T(8,128)(2,1)}) custom-call(bf16[512,384]{1,0:T(8,128)(2,1)} %q_in.1, bf16[512,384]{1,0:T(8,128)(2,1)} %k_in.1, bf16[512,384]{1,0:T(8,128)(2,1)} %v_in.1, f32[384]{0:T(512)} %qg_in.1, ...), custom_call_target="tpu_custom_call" | custom-call | flops 8000000000 | bytes 4200000 | tf_op jit(solution)/shard_map/pallas_call | solution.py:532
  80.6 2.5 %shard_map.111 = (bf16[512,768]{1,0:T(8,128)(2,1)}, bf16[512,384]{1,0:T(8,128)(2,1)}, bf16[512,384]{1,0:T(8,128)(2,1)}, bf16[512,384]{1,0:T(8,128)(2,1)}, bf16[96,768]{1,0:T(8,128)(2,1)}) custom-call(bf16[512,768]{1,0:T(8,128)(2,1)} %get-tuple-element.10.refs_0_, bf16[512,384]{1,0:T(8,128)(2,1)} %get-tuple-element.11.refs_1_, ...), custom_call_target="tpu_custom_call" | custom-call | tf_op jit(solution)/shard_map/pallas_call | solution.py:545

commit v3 on v2

--- a/solution.py
+++ b/solution.py
@@ -13,8 +13,8 @@
 HALF_ROWS = 48
 HALF_COLS = 384
 TILE_ROWS = 128
-PART_SLOTS = (((2, 5), (6, 7)), ((7, 8), (9, 12)))
-PART_SHIFT = (3, 8)
+PART_SLOTS = ((1, 2, 3, 5), (6, 7, 8, 10))
+SCATTER_SLOTS = (0, 4, 9, 11, 13)
 STORE_PARTS = 2
 EPSILON = 1e-06
 MESH = pl.DeviceIdType.MESH
@@ -61,8 +61,8 @@
     def y_turn(j):
         return device(lax.rem(y + 1 + 2 * j, NY), x, core, z)
 
-    def z_turn(image):
-        return (row, lax.rem(z + 1 + 6 * image, NZ))
+    def z_turn(way):
+        return (row, lax.rem(z + 1 + 6 * way, NZ))
 
     sibling = device(y, x, 1 - core, z)
 
@@ -153,15 +153,21 @@
                 ws1_copy(i, j, s).wait_send()
                 ws2_copy(i, j, s).wait_send()
 
-    def a_copy(image, s, h):
-        origin = lax.rem(z + (NZ - s if image == 0 else s), NZ)
-        ref = aall.at[origin * HEADS_HERE + h, pl.ds(image * PATCHES, PATCHES)]
-        return remote(ref, ref, a_send.at[image, s, h], a_recv.at[image, s, h], z_turn(image))
-
-    def a_pass(s, h):
-        for image in range(2):
-            a_copy(image, s - 1, h).wait_recv()
-            a_copy(image, s, h).start()
+    def image_rows(image):
+        return pl.ds(pl.multiple_of(image * PATCHES, PATCHES), PATCHES)
+
+    def a_copy(way, s, image, h):
+        origin = lax.rem(z + (NZ - s if way == 0 else s), NZ)
+        ref = aall.at[origin * HEADS_HERE + h, image_rows(image)]
+        return remote(ref, ref, a_send.at[way, s, image, h], a_recv.at[way, s, image, h], z_turn(way))
+
+    def a_own(image, h):
+        for way in range(2):
+            a_copy(way, 0, image, h).start()
+
+    def a_pass(way, s, image, h):
+        a_copy(way, s - 1, image, h).wait_recv()
+        a_copy(way, s, image, h).start()
 
     def head_slice(image, h):
         return (pl.ds(image * PATCHES, PATCHES), pl.ds(pl.multiple_of(h * HEAD_DIM, HEAD_DIM), HEAD_DIM))
@@ -212,27 +218,30 @@
         piece = wall[j, lax.div(o, 2), pl.ds(2 * lax.rem(o, 2), 2)]
         return piece.reshape(HEADS_HERE * HEAD_DIM, HALF_COLS)
 
-    def g_copy(image, s, h):
-        return remote(
-            gsend.at[image, s, h], grecv.at[image, s, h], g_send.at[image, s, h], g_recv.at[image, s, h], z_turn(image)
+    def g_copy(way, s, image, h):
+        at = (way, s, image, h)
+        return remote(gsend.at[at], grecv.at[at], g_send.at[at], g_recv.at[at], z_turn(way))
+
+    def g_term(owner):
+        return dot_nt(ct_ref[:, :HALF_COLS], weight_rows(0, owner)) + dot_nt(
+            ct_ref[:, HALF_COLS:], weight_rows(1, owner)
         )
 
-    def g_term(image, s):
-        owner = lax.rem(z + (2 * NZ - 1 - s if image == 0 else 1 + s), NZ)
-        rows = pl.ds(image * PATCHES, PATCHES)
-        return dot_nt(ct_ref[rows, :HALF_COLS], weight_rows(0, owner)) + dot_nt(
-            ct_ref[rows, HALF_COLS:], weight_rows(1, owner)
-        )
-
-    def head_columns(value, h):
-        return value[:, h * HEAD_DIM : (h + 1) * HEAD_DIM]
-
-    def g_first():
+    def g_part(term, image, h):
+        return term[image * PATCHES : (image + 1) * PATCHES, h * HEAD_DIM : (h + 1) * HEAD_DIM]
+
+    def g_owner(way, s):
+        return lax.rem(z + (NZ + 4 - s if way == 0 else 4 + s), NZ)
+
+    def g_make_term(way, s):
+        term = g_term(g_owner(way, s))
         for image in range(2):
-            term = g_term(image, 0)
             for h in range(HEADS_HERE):
-                gsend[image, 0, h] = head_columns(term, h).astype(BF16)
-                g_copy(image, 0, h).start()
+                gterm[s % 2, way, image, h] = g_part(term, image, h)
+
+    def g_fresh(way, s, image, h, value):
+        gsend[way, s, image, h] = value.astype(BF16)
+        g_copy(way, s, image, h).start()
 
     def gw_copy(index, o):
         place = pl.ds(2 * lax.rem(o, 2), 2)
@@ -246,8 +255,9 @@
 
     def gw_block(index, o):
         panel = jnp.concatenate([aall[o * HEADS_HERE + h] for h in range(HEADS_HERE)], axis=1)
+        product = dot_tn(panel, ct_ref[...]).astype(BF16)
         for j in range(2):
-            value = dot_tn(panel, ct_ref[:, j * HALF_COLS : (j + 1) * HALF_COLS]).astype(BF16)
+            value = product[:, j * HALF_COLS : (j + 1) * HALF_COLS]
             for xx in range(2):
                 for cc in range(2):
                     for i in range(2):
@@ -263,40 +273,52 @@
             return gwb[core, :, d, i, j].astype(F32) + sib[:, d, i, j].astype(F32)
         return gwb[core, d, :, i, j].astype(F32) + sib[d, :, i, j].astype(F32)
 
-    def p1_copy(i, j, s):
-        peer = x_turn(j) if i == 0 else y_turn(j)
-        return remote(s1.at[i, j, s], r1.at[i, j, s], p1_send.at[i, j, s], p1_recv.at[i, j, s], peer)
-
-    def p2_copy(i, j, s):
-        peer = y_turn(j) if i == 0 else x_turn(j)
-        return remote(s2.at[i, j, s], r2.at[i, j, s], p2_send.at[i, j, s], p2_recv.at[i, j, s], peer)
+    def p1_copy(i, j, n):
+        turn = 1 - j if n == 1 else j
+        peer = x_turn(turn) if i == 0 else y_turn(turn)
+        return remote(s1.at[i, j, n], r1.at[i, j, n], p1_send.at[i, j, n], p1_recv.at[i, j, n], peer)
+
+    def p2_copy(i, j, n):
+        turn = 1 - j if n == 1 else j
+        peer = y_turn(turn) if i == 0 else x_turn(turn)
+        return remote(s2.at[i, j, n], r2.at[i, j, n], p2_send.at[i, j, n], p2_recv.at[i, j, n], peer)
 
     def scatter_step(t):
+        if t == 0:
+            for n in range(2):
+                for i, j in quarters:
+                    s1[i, j, n] = chip_sum(i, j, behind(x if i == 0 else y, 2 - n, j)).astype(BF16)
+                    p1_copy(i, j, n).start()
+            return
         for i, j in quarters:
             first, second = (x, y) if i == 0 else (y, x)
-            if t <= 3:
-                total = chip_sum(i, j, behind(first, (1 + t) % 4, j))
-                if t > 0:
-                    p1_copy(i, j, t - 1).wait_recv()
-                    total = total + r1[i, j, t - 1].astype(F32)
-                if t < 3:
-                    s1[i, j, t] = total.astype(BF16)
-                    p1_copy(i, j, t).start()
-                else:
-                    c1[i, j] = total
-                    s2[i, j, 0] = c1[i, j, behind(second, 1, j)].astype(BF16)
-                    p2_copy(i, j, 0).start()
+            if t == 1:
+                p1_copy(i, j, 0).wait_recv()
+                total = chip_sum(i, j, behind(first, 3, j)) + r1[i, j, 0].astype(F32)
+                s1[i, j, 2] = total.astype(BF16)
+                p1_copy(i, j, 2).start()
+            elif t == 2:
+                total = chip_sum(i, j, first)
+                for n in (1, 2):
+                    p1_copy(i, j, n).wait_recv()
+                    total = total + r1[i, j, n].astype(F32)
+                c1[i, j] = total
+                for n in range(2):
+                    s2[i, j, n] = c1[i, j, behind(second, 2 - n, j)].astype(BF16)
+                    p2_copy(i, j, n).start()
+            elif t == 3:
+                p2_copy(i, j, 0).wait_recv()
+                total = c1[i, j, behind(second, 3, j)] + r2[i, j, 0].astype(F32)
+                s2[i, j, 2] = total.astype(BF16)
+                p2_copy(i, j, 2).start()
             else:
-                s = t - 4
-                p2_copy(i, j, s).wait_recv()
-                total = c1[i, j, behind(second, (2 + s) % 4, j)] + r2[i, j, s].astype(F32)
-                if s < 2:
-                    s2[i, j, s + 1] = total.astype(BF16)
-                    p2_copy(i, j, s + 1).start()
-                else:
-                    gw_ref[
-                        i * HALF_ROWS : (i + 1) * HALF_ROWS, j * HALF_COLS : (j + 1) * HALF_COLS
-                    ] = total.astype(BF16)
+                total = c1[i, j, second]
+                for n in (1, 2):
+                    p2_copy(i, j, n).wait_recv()
+                    total = total + r2[i, j, n].astype(F32)
+                gw_ref[
+                    i * HALF_ROWS : (i + 1) * HALF_ROWS, j * HALF_COLS : (j + 1) * HALF_COLS
+                ] = total.astype(BF16)
 
     def output_copy(tile):
         rows = pl.ds(pl.multiple_of(tile * TILE_ROWS, TILE_ROWS), TILE_ROWS)
@@ -320,17 +342,24 @@
             for n, (source, target) in enumerate(((gq_ref, gq_hbm), (gk_ref, gk_hbm), (gv_ref, gv_hbm)))
         ]
 
+    def gw_result():
+        return pltpu.make_async_copy(gw_ref, gw_hbm, gw_sem)
+
+    for load in loads[:3]:
+        load.wait()
+    forward(0, 0)
+    pl.semaphore_wait(barrier, 7)
+    a_own(0, 0)
     loads[3].wait()
     for i, j in quarters:
         wall[j, y, x, core, i] = w_ref[
             i * HALF_ROWS : (i + 1) * HALF_ROWS, j * HALF_COLS : (j + 1) * HALF_COLS
         ]
-    for load in loads[:3]:
-        load.wait()
-    pl.semaphore_wait(barrier, 7)
     for i, j in quarters:
         w1_copy(i, j, 0).start()
     ws0_copy().start()
+    forward(1, 0)
+    a_own(1, 0)
 
     def at_slot(slot, moments, action):
         for t, moment in moments:
@@ -338,125 +367,161 @@
             def _():
                 action(t)
 
+    def at_slot_of(slot, moments, action):
+        hit, tile = slot == moments[0], jnp.where(slot == moments[0], 0, 0)
+        for n, moment in enumerate(moments[1:]):
+            hit, tile = jnp.logical_or(hit, slot == moment), jnp.where(slot == moment, n + 1, tile)
+
+        @pl.when(hit)
+        def _():
+            action(tile)
+
     def forward_loop(h, carry):
         for image in range(2):
             forward(image, h)
-            a_copy(image, 0, h).start()
+            a_own(image, h)
         at_slot(h, ((0, 1), (1, 2)), weight_step)
-
-        @pl.when(h >= 1)
-        def _():
-            a_pass(1, h - 1)
-
         return carry
 
-    lax.fori_loop(0, HEADS_HERE, forward_loop, 0)
+    lax.fori_loop(1, HEADS_HERE, forward_loop, 0)
     loads[4].wait()
-    a_pass(1, HEADS_HERE - 1)
-    gw_block(0, gw_owner(0))
+
+    def block(index):
+        gw_block(index, gw_owner(index))
 
     def gather_loop(slot, carry):
-        a_pass(2 + lax.div(slot, HEADS_HERE), lax.rem(slot, HEADS_HERE))
-        at_slot(slot, ((2, 0), (3, 4), (4, 8), (5, 12)), weight_step)
-
-        @pl.when(jnp.logical_or(slot == 9, jnp.logical_or(slot == 11, jnp.logical_or(slot == 13, slot == 14))))
-        def _():
-            index = jnp.where(slot == 9, 4, jnp.where(slot == 11, 3, jnp.where(slot == 13, 5, 2)))
-            gw_block(index, gw_owner(index))
+        k = lax.rem(slot, 6)
+        for s in (1, 2):
+            @pl.when(lax.div(slot, 6) == s - 1)
+            def _():
+                for way in range(2):
+                    a_pass(way, s, lax.rem(k, 2), lax.div(k, 2))
+
+        at_slot(slot, ((2, 1), (3, 4), (4, 7), (5, 10)), weight_step)
+
+        @pl.when(jnp.logical_or(slot == 2, jnp.logical_or(slot == 6, slot == 8)))
+        def _():
+            block(jnp.where(slot == 2, 0, jnp.where(slot == 6, 1, 7)))
 
         return carry
 
-    lax.fori_loop(0, 5 * HEADS_HERE, gather_loop, 0)
+    lax.fori_loop(0, 12, gather_loop, 0)
+
+    def last_hop_loop(h, carry):
+        for way in range(2):
+            a_pass(way, 3, way, h)
+
+        @pl.when(h < 2)
+        def _():
+            block(2 + 4 * h)
+
+        return carry
+
+    lax.fori_loop(0, HEADS_HERE, last_hop_loop, 0)
     weight_wait()
-    g_first()
+    term = g_term(g_owner(0, 0))
     for h in range(HEADS_HERE):
-        for image in range(2):
-            a_copy(image, 6, h).wait_recv()
-
-    def last_three(n, carry):
-        index = jnp.where(n == 0, 6, jnp.where(n == 1, 1, 7))
-        gw_block(index, gw_owner(index))
+        for way in range(2):
+            g_fresh(way, 0, way, h, g_part(term, way, h))
+    for h in range(HEADS_HERE):
+        for way in range(2):
+            a_copy(way, 2, 1 - way, h).wait_recv()
+
+    def third_hop_loop(n, carry):
+        block(3 + 2 * n)
         return carry
 
-    lax.fori_loop(0, 3, last_three, 0)
+    lax.fori_loop(0, 2, third_hop_loop, 0)
+    for way in range(2):
+        g_make_term(way, 1)
+    for h in range(HEADS_HERE):
+        for way in range(2):
+            g_fresh(way, 1, 1 - way, h, gterm[1, way, 1 - way, h])
+    for h in range(HEADS_HERE):
+        for way in range(2):
+            a_copy(way, 3, way, h).wait_recv()
+    block(4)
 
     def reduce_loop(slot, carry):
-        s, h = 1 + lax.div(slot, HEADS_HERE), lax.rem(slot, HEADS_HERE)
-
-        @pl.when(h == 0)
-        def _():
-            for image in range(2):
-                term = g_term(image, s)
-                for head in range(HEADS_HERE):
-                    gterm[image, head] = head_columns(term, head)
-
-        for image in range(2):
-            g_copy(image, s - 1, h).wait_recv()
-            total = gterm[image, h] + grecv[image, s - 1, h].astype(F32)
-            gsend[image, s, h] = total.astype(BF16)
-            g_copy(image, s, h).start()
-
-        @pl.when(slot == 1)
+        s, k = 1 + lax.div(slot + 3, 6), lax.rem(slot + 3, 6)
+        h = jnp.where(slot < 3, slot, lax.div(k, 2))
+        for way in range(2):
+            image = jnp.where(slot < 3, way, lax.rem(k, 2))
+            g_copy(way, s - 1, image, h).wait_recv()
+            total = gterm[lax.rem(s, 2), way, image, h] + grecv[way, s - 1, image, h].astype(F32)
+            g_fresh(way, s, image, h, total)
+
+        @pl.when(slot == SCATTER_SLOTS[0])
         def _():
             for index in range(NZ):
                 gw_copy(index, gw_owner(index)).wait_recv()
 
-        at_slot(slot, ((0, 1), (1, 5), (2, 8), (3, 12), (4, 14), (5, 16)), scatter_step)
+        at_slot(slot, tuple(enumerate(SCATTER_SLOTS)), scatter_step)
+        for moment, way, step in ((1, 0, 2), (2, 1, 2), (5, 0, 3), (7, 1, 3), (11, 0, 4)):
+            @pl.when(slot == moment)
+            def _():
+                g_make_term(way, step)
+
         for j in range(2):
-
-            @pl.when(jnp.logical_or(*[jnp.logical_and(slot >= a, slot < b) for a, b in PART_SLOTS[j]]))
-            def _():
-                output_part(slot - jnp.where(slot >= PART_SLOTS[j][1][0], PART_SHIFT[j], PART_SLOTS[j][0][0]), j)
+            at_slot_of(slot, PART_SLOTS[j], lambda tile: output_part(tile, j))
+
+        @pl.when(slot == SCATTER_SLOTS[4])
+        def _():
+            gw_result().start()
+            for i, j in quarters:
+                for n in range(3):
+                    p1_copy(i, j, n).wait_send()
+            for index in range(NZ):
+                gw_copy(index, gw_owner(index)).wait_send()
+
+        @pl.when(slot == 10)
+        def _():
+            weight_sent()
+
+        @pl.when(slot == 12)
+        def _():
+            for way, s, image, h in gather_chunks:
+                a_copy(way, s, image, h).wait_send()
+
+        @pl.when(slot == 14)
+        def _():
+            for way, s, image, h in reduce_chunks:
+                if s < 2:
+                    g_copy(way, s, image, h).wait_send()
 
         return carry
 
-    lax.fori_loop(0, 6 * HEADS_HERE, reduce_loop, 0)
-
-    for image in range(2):
-        term = g_term(image, 7)
-        for head in range(HEADS_HERE):
-            gterm[image, head] = head_columns(term, head)
+    chunks = [(way, image, h) for way in range(2) for image in range(2) for h in range(HEADS_HERE)]
+    gather_chunks = [(way, s, image, h) for s in range(4) for way, image, h in chunks if s < 3 or way == image]
+    reduce_chunks = [(way, s, image, h) for s in range(4) for way, image, h in chunks if s > 0 or way == image]
+    lax.fori_loop(0, 15, reduce_loop, 0)
 
     def backward_loop(h, carry):
         for image in range(2):
-            g_copy(image, 6, h).wait_recv()
-            grad_attended = (gterm[image, h] + grecv[image, 6, h].astype(F32)).astype(BF16)
-            backward(image, h, grad_attended)
+            total = gterm[0, 0, image, h]
+            for way in range(2):
+                g_copy(way, 3, image, h).wait_recv()
+                total = total + grecv[way, 3, image, h].astype(F32)
+            backward(image, h, total.astype(BF16))
         for copy in grad_copies(h):
             copy.start()
 
-        @pl.when(h == 0)
-        def _():
-            scatter_step(6)
-            gw_result = pltpu.make_async_copy(gw_ref, gw_hbm, gw_sem)
-            gw_result.start()
-
         return carry
 
     lax.fori_loop(0, HEADS_HERE, backward_loop, 0)
+
+    for way, s, image, h in reduce_chunks:
+        if s >= 2:
+            g_copy(way, s, image, h).wait_send()
+    for i, j in quarters:
+        for s in range(3):
+            p2_copy(i, j, s).wait_send()
+    for tile in range(4):
+        output_copy(tile).wait()
+    gw_result().wait()
     for h in range(HEADS_HERE):
         for copy in grad_copies(h):
             copy.wait()
-    pltpu.make_async_copy(gw_ref, gw_hbm, gw_sem).wait()
-    for tile in range(4):
-        output_copy(tile).wait()
-
-    weight_sent()
-    for i, j in quarters:
-        for s in range(3):
-            p1_copy(i, j, s).wait_send()
-            p2_copy(i, j, s).wait_send()
-    for index in range(NZ):
-        gw_copy(index, gw_owner(index)).wait_send()
-
-    def sent_loop(s, carry):
-        for h in range(HEADS_HERE):
-            for image in range(2):
-                a_copy(image, s, h).wait_send()
-                g_copy(image, s, h).wait_send()
-        return carry
-
-    lax.fori_loop(0, 7, sent_loop, 0)
 
 
 def store_kernel(*refs):
@@ -502,9 +567,9 @@
         pltpu.VMEM(unit, F32),
         pltpu.VMEM(unit, BF16),
         pltpu.VMEM(unit, BF16),
-        pltpu.VMEM((2, 7, HEADS_HERE, PATCHES, HEAD_DIM), BF16),
-        pltpu.VMEM((2, 7, HEADS_HERE, PATCHES, HEAD_DIM), BF16),
-        pltpu.VMEM(unit, F32),
+        pltpu.VMEM((2, 4) + unit, BF16),
+        pltpu.VMEM((2, 4) + unit, BF16),
+        pltpu.VMEM((2, 2) + unit, F32),
         pltpu.VMEM((2, NY, NX, 2, 2) + quarter, BF16),
         pltpu.VMEM((NY, NX, 2, 2) + quarter, BF16),
         pltpu.VMEM((2, 2, 3, 4) + quarter, BF16),
@@ -513,7 +578,7 @@
         pltpu.VMEM((2, 2, 3) + quarter, BF16),
         pltpu.VMEM((2, 2, 4) + quarter, F32),
     ]
-    ring4, ring8 = (2, 2, 3), (2, 7, HEADS_HERE)
+    ring4, ring8 = (2, 2, 3), (2, 4, 2, HEADS_HERE)
     scratch += [dma((5,)), dma((4,)), dma((3, HEADS_HERE)), dma]
     scratch += [dma(ring4), dma(ring4), dma(ring4), dma(ring4), dma, dma]
     scratch += [dma(ring4), dma(ring4), dma(ring4), dma(ring4)]

time: 84.6 us -> 78.6 us (0.929); the launches traced: 83.1 us -> 78.4 us
  Pallas kernels: 82.4 us -> 77.8 us
    pallas_call x1, Pallas kernels: 80 us -> 75.3 us  [per_device(): pl.pallas_call(block_kernel, out_shape=results, in_specs=[anywhere] * 3 +...]
where the time goes in v3:
time: 78.6 us; the launch traced here: 78.4 us
  Pallas kernels  77.8 us (99%)
    pallas_call x1, Pallas kernels, per_device(): pl.pallas_call(block_kernel, out_shape=results, in_specs=[anywhere] * 3 +...  75.3 us
    pallas_call x1, Pallas kernels, per_device(): pl.pallas_call(store_kernel, out_shape=results, in_specs=[anywhere] * 5,...  2.48 us

profile of v3, /device:TPU:1, one launch (start us, length us, event | category | flops | bytes accessed | tf_op | source)
XLA Modules:
  0.0 78.4 jit_solution(10067084107620801844)
XLA Ops:
  0.6 75.3 %shard_map.110 = (bf16[512,768]{1,0:T(8,128)(2,1)}, bf16[512,384]{1,0:T(8,128)(2,1)}, bf16[512,384]{1,0:T(8,128)(2,1)}, bf16[512,384]{1,0:T(8,128)(2,1)}, bf16[96,768]{1,0:T(8,128)(2,1)}) custom-call(bf16[512,384]{1,0:T(8,128)(2,1)} %q_in.1, bf16[512,384]{1,0:T(8,128)(2,1)} %k_in.1, bf16[512,384]{1,0:T(8,128)(2,1)} %v_in.1, f32[384]{0:T(512)} %qg_in.1, ...), custom_call_target="tpu_custom_call" | custom-call | flops 8000000000 | bytes 4200000 | tf_op jit(solution)/shard_map/pallas_call | solution.py:597
  75.9 2.5 %shard_map.111 = (bf16[512,768]{1,0:T(8,128)(2,1)}, bf16[512,384]{1,0:T(8,128)(2,1)}, bf16[512,384]{1,0:T(8,128)(2,1)}, bf16[512,384]{1,0:T(8,128)(2,1)}, bf16[96,768]{1,0:T(8,128)(2,1)}) custom-call(bf16[512,768]{1,0:T(8,128)(2,1)} %get-tuple-element.10.refs_0_, bf16[512,384]{1,0:T(8,128)(2,1)} %get-tuple-element.11.refs_1_, ...), custom_call_target="tpu_custom_call" | custom-call | tf_op jit(solution)/shard_map/pallas_call | solution.py:610

commit v4 on v3

--- a/solution.py
+++ b/solution.py
@@ -165,9 +165,10 @@
         for way in range(2):
             a_copy(way, 0, image, h).start()
 
-    def a_pass(way, s, image, h):
-        a_copy(way, s - 1, image, h).wait_recv()
-        a_copy(way, s, image, h).start()
+    def a_pair(way, s, h):
+        origin = lax.rem(z + (NZ - s if way == 0 else s), NZ)
+        ref = aall.at[origin * HEADS_HERE + h]
+        return remote(ref, ref, a_send.at[way, s, 0, h], a_recv.at[way, s, 0, h], z_turn(way))
 
     def head_slice(image, h):
         return (pl.ds(image * PATCHES, PATCHES), pl.ds(pl.multiple_of(h * HEAD_DIM, HEAD_DIM), HEAD_DIM))
@@ -394,8 +395,16 @@
         for s in (1, 2):
             @pl.when(lax.div(slot, 6) == s - 1)
             def _():
-                for way in range(2):
-                    a_pass(way, s, lax.rem(k, 2), lax.div(k, 2))
+                @pl.when(lax.rem(k, 2) == 0)
+                def _():
+                    h = lax.div(k, 2)
+                    for way in range(2):
+                        if s == 1:
+                            for image in range(2):
+                                a_copy(way, 0, image, h).wait_recv()
+                        else:
+                            a_pair(way, 1, h).wait_recv()
+                        a_pair(way, s, h).start()
 
         at_slot(slot, ((2, 1), (3, 4), (4, 7), (5, 10)), weight_step)
 
@@ -409,7 +418,8 @@
 
     def last_hop_loop(h, carry):
         for way in range(2):
-            a_pass(way, 3, way, h)
+            a_pair(way, 2, h).wait_recv()
+            a_copy(way, 3, way, h).start()
 
         @pl.when(h < 2)
         def _():
@@ -423,10 +433,6 @@
     for h in range(HEADS_HERE):
         for way in range(2):
             g_fresh(way, 0, way, h, g_part(term, way, h))
-    for h in range(HEADS_HERE):
-        for way in range(2):
-            a_copy(way, 2, 1 - way, h).wait_recv()
-
     def third_hop_loop(n, carry):
         block(3 + 2 * n)
         return carry
@@ -481,7 +487,10 @@
         @pl.when(slot == 12)
         def _():
             for way, s, image, h in gather_chunks:
-                a_copy(way, s, image, h).wait_send()
+                if s in (0, 3):
+                    a_copy(way, s, image, h).wait_send()
+                elif image == 0:
+                    a_pair(way, s, h).wait_send()
 
         @pl.when(slot == 14)
         def _():
@@ -506,19 +515,28 @@
         for copy in grad_copies(h):
             copy.start()
 
+        @pl.when(h == 0)
+        def _():
+            for way, s, image, head in reduce_chunks:
+                if s == 2:
+                    g_copy(way, s, image, head).wait_send()
+
+        @pl.when(h == 1)
+        def _():
+            for i, j in quarters:
+                for n in range(3):
+                    p2_copy(i, j, n).wait_send()
+            for tile in range(4):
+                output_copy(tile).wait()
+            gw_result().wait()
+
         return carry
 
     lax.fori_loop(0, HEADS_HERE, backward_loop, 0)
 
     for way, s, image, h in reduce_chunks:
-        if s >= 2:
+        if s == 3:
             g_copy(way, s, image, h).wait_send()
-    for i, j in quarters:
-        for s in range(3):
-            p2_copy(i, j, s).wait_send()
-    for tile in range(4):
-        output_copy(tile).wait()
-    gw_result().wait()
     for h in range(HEADS_HERE):
         for copy in grad_copies(h):
             copy.wait()

time: 78.6 us -> 78.2 us (level)
  no operation moved by 1% of the time
where the time goes in v4:
time: 78.2 us; the launch traced here: 78 us
  Pallas kernels  77.4 us (99%)
    pallas_call x1, Pallas kernels, per_device(): pl.pallas_call(block_kernel, out_shape=results, in_specs=[anywhere] * 3 +...  74.9 us
    pallas_call x1, Pallas kernels, per_device(): pl.pallas_call(store_kernel, out_shape=results, in_specs=[anywhere] * 5,...  2.48 us

profile of v4, /device:TPU:1, one launch (start us, length us, event | category | flops | bytes accessed | tf_op | source)
XLA Modules:
  0.0 78.0 jit_solution(1356173092982919636)
XLA Ops:
  0.6 74.9 %shard_map.110 = (bf16[512,768]{1,0:T(8,128)(2,1)}, bf16[512,384]{1,0:T(8,128)(2,1)}, bf16[512,384]{1,0:T(8,128)(2,1)}, bf16[512,384]{1,0:T(8,128)(2,1)}, bf16[96,768]{1,0:T(8,128)(2,1)}) custom-call(bf16[512,384]{1,0:T(8,128)(2,1)} %q_in.1, bf16[512,384]{1,0:T(8,128)(2,1)} %k_in.1, bf16[512,384]{1,0:T(8,128)(2,1)} %v_in.1, f32[384]{0:T(512)} %qg_in.1, ...), custom_call_target="tpu_custom_call" | custom-call | flops 8000000000 | bytes 4200000 | tf_op jit(solution)/shard_map/pallas_call | solution.py:615
  75.5 2.5 %shard_map.111 = (bf16[512,768]{1,0:T(8,128)(2,1)}, bf16[512,384]{1,0:T(8,128)(2,1)}, bf16[512,384]{1,0:T(8,128)(2,1)}, bf16[512,384]{1,0:T(8,128)(2,1)}, bf16[96,768]{1,0:T(8,128)(2,1)}) custom-call(bf16[512,768]{1,0:T(8,128)(2,1)} %get-tuple-element.10.refs_0_, bf16[512,384]{1,0:T(8,128)(2,1)} %get-tuple-element.11.refs_1_, ...), custom_call_target="tpu_custom_call" | custom-call | tf_op jit(solution)/shard_map/pallas_call | solution.py:628

commit v5 on v4

--- a/solution.py
+++ b/solution.py
@@ -380,7 +380,8 @@
     def forward_loop(h, carry):
         for image in range(2):
             forward(image, h)
-            a_own(image, h)
+        for way in range(2):
+            a_pair(way, 0, h).start()
         at_slot(h, ((0, 1), (1, 2)), weight_step)
         return carry
 
@@ -400,8 +401,14 @@
                     h = lax.div(k, 2)
                     for way in range(2):
                         if s == 1:
-                            for image in range(2):
-                                a_copy(way, 0, image, h).wait_recv()
+                            @pl.when(h == 0)
+                            def _():
+                                for image in range(2):
+                                    a_copy(way, 0, image, 0).wait_recv()
+
+                            @pl.when(h > 0)
+                            def _():
+                                a_pair(way, 0, h).wait_recv()
                         else:
                             a_pair(way, 1, h).wait_recv()
                         a_pair(way, s, h).start()
@@ -487,7 +494,7 @@
         @pl.when(slot == 12)
         def _():
             for way, s, image, h in gather_chunks:
-                if s in (0, 3):
+                if s == 3 or (s == 0 and h == 0):
                     a_copy(way, s, image, h).wait_send()
                 elif image == 0:
                     a_pair(way, s, h).wait_send()

time: 78.2 us -> 78.2 us (level)
  no operation moved by 1% of the time
where the time goes in v5:
time: 78.2 us; the launch traced here: 78 us
  Pallas kernels  77.4 us (99%)
    pallas_call x1, Pallas kernels, per_device(): pl.pallas_call(block_kernel, out_shape=results, in_specs=[anywhere] * 3 +...  74.9 us
    pallas_call x1, Pallas kernels, per_device(): pl.pallas_call(store_kernel, out_shape=results, in_specs=[anywhere] * 5,...  2.48 us

profile of v5, /device:TPU:1, one launch (start us, length us, event | category | flops | bytes accessed | tf_op | source)
XLA Modules:
  0.0 78.0 jit_solution(4843827398369720586)
XLA Ops:
  0.6 74.9 %shard_map.110 = (bf16[512,768]{1,0:T(8,128)(2,1)}, bf16[512,384]{1,0:T(8,128)(2,1)}, bf16[512,384]{1,0:T(8,128)(2,1)}, bf16[512,384]{1,0:T(8,128)(2,1)}, bf16[96,768]{1,0:T(8,128)(2,1)}) custom-call(bf16[512,384]{1,0:T(8,128)(2,1)} %q_in.1, bf16[512,384]{1,0:T(8,128)(2,1)} %k_in.1, bf16[512,384]{1,0:T(8,128)(2,1)} %v_in.1, f32[384]{0:T(512)} %qg_in.1, ...), custom_call_target="tpu_custom_call" | custom-call | flops 8000000000 | bytes 4200000 | tf_op jit(solution)/shard_map/pallas_call | solution.py:622
  75.5 2.5 %shard_map.111 = (bf16[512,768]{1,0:T(8,128)(2,1)}, bf16[512,384]{1,0:T(8,128)(2,1)}, bf16[512,384]{1,0:T(8,128)(2,1)}, bf16[512,384]{1,0:T(8,128)(2,1)}, bf16[96,768]{1,0:T(8,128)(2,1)}) custom-call(bf16[512,768]{1,0:T(8,128)(2,1)} %get-tuple-element.10.refs_0_, bf16[512,384]{1,0:T(8,128)(2,1)} %get-tuple-element.11.refs_1_, ...), custom_call_target="tpu_custom_call" | custom-call | tf_op jit(solution)/shard_map/pallas_call | solution.py:635
